TPU v7x, 256 devices: a whole 4x4x8 slice. The times are simulated.
256 devices in a mesh: dp: 32 (over x_hi, z, core), param: 8 (over y, x_lo).
Axes of the slice: x: 4 (x_hi: 2, x_lo: 2; x = x_hi * 2 + x_lo), y: 4, z: 8, core: 2. Of those that a mesh axis runs over, the one named last changes fastest.
Arguments:
- conv_input: bfloat16 [65536, 1024], P(('dp', 'param')), may hold values from -6 to 6
- block_dest: int32 [8192, 1], P(('dp', 'param')), may hold values from 0 to 31; in each aligned block of 32 rows (0 to 31, 32 to 63, ...) at most 2 rows name the same one
- live_frames: int32 [8192], P(('dp', 'param')), may hold values from 1 to 8
- conv_weight: bfloat16 [1024, 512], P('param'), may hold values from -0.1875 to 0.1875
- conv_gain: float32 [512], replicated, may hold values from 0.1 to 1.9
- conv_shift: float32 [512], replicated, may hold values from -3 to 3
- feat_gain: float32 [512], replicated, may hold values from 0.1 to 1.9
- feat_shift: float32 [512], replicated, may hold values from -3 to 3
- proj_weight: bfloat16 [512, 1920], P('param'), may hold values from -0.25 to 0.25
- proj_bias: float32 [1920], replicated, may hold values from -3 to 3
- cotangent: bfloat16 [131072, 1920], P(('dp', 'param')), may hold values from -6 to 6
Outputs:
- projected: float32 [131072, 1920], P(('dp', 'param'))
- frames_grad: float32 [65536, 1024], P(('dp', 'param'))
- conv_weight_grad: float32 [1024, 512], P('param')
- proj_weight_grad: float32 [512, 1920], P('param')
- norm_grads: float32 [4, 512], replicated
- bias_grad: float32 [1920], replicated
Inputs may be any that keep to these rules, and one draw needn't show every extreme that they name: `block_dest`: each device sends at most 2 of its 32 segments to one index of dp, and some device sends exactly 2 to one.
All inputs are finite; a program needn't handle non-finite values.
Results may differ from a plain program's by a relative error of at most 0.003.
Values may be sent and summed in bfloat16 or wider, within the bound.
A program may use at most 64 MiB of HBM per device.

v0:
```python
import math

import jax
import jax.numpy as jnp
from jax import lax
from jax.sharding import PartitionSpec as P

CAP = 2


epsilon = 1e-05


def normalize(values, factor, offset):
    average = jnp.mean(values, axis=-1, keepdims=True)
    centred = values - average
    spread = jnp.mean(centred * centred, axis=-1, keepdims=True)
    return centred * lax.rsqrt(spread + epsilon) * factor + offset


def encode_tail(hidden, conv_gain, conv_shift, feat_gain, feat_shift):
    active = jax.nn.gelu(normalize(hidden, conv_gain, conv_shift), approximate=False)
    return normalize(active, feat_gain, feat_shift)


def contract_rows(left, right):
    return lax.dot_general(
        left, right, (((0,), (0,)), ((), ())), preferred_element_type=jnp.float32
    )


def contract_cols(left, right):
    return lax.dot_general(
        left, right, (((1,), (1,)), ((), ())), preferred_element_type=jnp.float32
    )


def place_exact(table, values):
    return jnp.dot(
        table, values, precision=lax.Precision.HIGHEST, preferred_element_type=jnp.float32
    )


def slot_table(destination, dp_count):
    onehot = (destination[:, None] == jnp.arange(dp_count, dtype=jnp.int32)[None, :]).astype(
        jnp.int32
    )
    earlier = jnp.cumsum(onehot, axis=0, dtype=jnp.int32) - onehot
    order_rank = jnp.sum(earlier * onehot, axis=1, dtype=jnp.int32)
    slot_index = destination * CAP + order_rank
    return slot_index[None, :] == jnp.arange(dp_count * CAP, dtype=jnp.int32)[:, None]


def project_forward(frame_rows, live_mask, conv_weight, proj_weight, proj_bias, norms):
    window = frame_rows
    hidden = jnp.dot(
        window,
        lax.all_gather(conv_weight, "param", axis=0, tiled=True),
        preferred_element_type=jnp.float32,
    )
    tail_out, pullback = jax.vjp(encode_tail, hidden, norms[0], norms[1], norms[2], norms[3])
    features = tail_out.astype(jnp.bfloat16)
    window = features
    lifted = jnp.dot(
        window,
        lax.all_gather(proj_weight, "param", axis=0, tiled=True),
        preferred_element_type=jnp.float32,
    )
    outputs = jnp.where(live_mask[:, None], lifted + proj_bias, 0.0)
    return (features, outputs, pullback)


def project_backward(
    frame_rows, features, pullback, upstream, conv_weight, proj_weight, grad_scale
):
    window = features
    proj_grad = lax.psum_scatter(
        contract_rows(window, upstream), "param", scatter_dimension=0, tiled=True
    )
    back_feat = contract_cols(upstream, lax.all_gather(proj_weight, "param", axis=0, tiled=True))
    grads = pullback(back_feat)
    hidden_back = grads[0].astype(jnp.bfloat16)
    window = frame_rows
    conv_grad = lax.psum_scatter(
        contract_rows(window, hidden_back), "param", scatter_dimension=0, tiled=True
    )
    back_rows = contract_cols(hidden_back, lax.all_gather(conv_weight, "param", axis=0, tiled=True))
    norm_local = jnp.stack([grads[1], grads[2], grads[3], grads[4]])
    bias_local = jnp.sum(upstream, axis=0, dtype=jnp.float32)
    replica = lax.psum((conv_grad, proj_grad), "dp")
    shared = lax.psum((norm_local, bias_local), ("dp", "param"))
    return (
        back_rows,
        replica[0] * grad_scale,
        replica[1] * grad_scale,
        shared[0] * grad_scale,
        shared[1] * grad_scale,
    )


def on_device(
    conv_input,
    block_dest,
    live_frames,
    conv_weight,
    conv_gain,
    conv_shift,
    feat_gain,
    feat_shift,
    proj_weight,
    proj_bias,
    cotangent,
):
    dp_count = lax.axis_size("dp")
    param_count = lax.axis_size("param")
    frames_dev, in_width = conv_input.shape
    segments = live_frames.shape[0]
    segment = frames_dev // segments
    grad_scale = 1.0 / math.sqrt(frames_dev * dp_count * param_count)
    norms = (conv_gain, conv_shift, feat_gain, feat_shift)
    placing = slot_table(block_dest[:, 0], dp_count)
    place_matrix = placing.astype(jnp.bfloat16)
    place_float = placing.astype(jnp.float32)
    position = jnp.arange(segment, dtype=jnp.int32)
    sending = jnp.dot(
        place_matrix,
        conv_input.reshape(segments, segment * in_width),
        preferred_element_type=jnp.float32,
    ).astype(jnp.bfloat16)
    slot_live = jnp.sum(
        jnp.where(placing, live_frames[None, :], 0), axis=1, dtype=jnp.int32
    ).reshape(dp_count, CAP)
    arrived, arrived_live = (
        lax.all_to_all(
            sending.reshape(dp_count, CAP * segment, in_width),
            "dp",
            split_axis=0,
            concat_axis=0,
            tiled=True,
        ),
        lax.all_to_all(slot_live, "dp", split_axis=0, concat_axis=0, tiled=True),
    )
    frame_rows = arrived.reshape(dp_count * CAP * segment, in_width)
    live_mask = (position[None, None, :] < arrived_live[:, :, None]).reshape(
        dp_count * CAP * segment
    )
    features, projected, pullback = project_forward(
        frame_rows, live_mask, conv_weight, proj_weight, proj_bias, norms
    )
    upstream = jnp.where(live_mask[:, None], cotangent, jnp.zeros_like(cotangent))
    back_rows, conv_weight_grad, proj_weight_grad, norm_grads, bias_grad = project_backward(
        frame_rows, features, pullback, upstream, conv_weight, proj_weight, grad_scale
    )
    returned = lax.all_to_all(
        back_rows.reshape(dp_count, CAP * segment, in_width),
        "dp",
        split_axis=0,
        concat_axis=0,
        tiled=True,
    )
    frames_grad = place_exact(
        place_float.T, returned.reshape(dp_count * CAP, segment * in_width)
    ).reshape(frames_dev, in_width)
    return (projected, frames_grad, conv_weight_grad, proj_weight_grad, norm_grads, bias_grad)


def solution(mesh):
    return jax.shard_map(
        on_device,
        mesh=mesh,
        in_specs=(
            P(("dp", "param"), None),
            P(("dp", "param"), None),
            P(("dp", "param")),
            P("param", None),
            P(),
            P(),
            P(),
            P(),
            P("param", None),
            P(),
            P(("dp", "param"), None),
        ),
        out_specs=(
            P(("dp", "param"), None),
            P(("dp", "param"), None),
            P("param", None),
            P("param", None),
            P(),
            P(),
        ),
        check_vma=False,
    )
```

profile of v0, /device:TPU:1, one launch (start us, length us, event | category | flops | bytes accessed | tf_op | source)
XLA Modules:
  0.0 574.1 jit_solution(17522901090263267413)
XLA Ops:
  11.6 12.6 %all-to-all-start = ((s32[32,1,2]{2,1,0:T(1,128)}), s32[32,1,2]{2,1,0:T(1,128)S(1)}, u32[]{:S(2)}, u32[]{:S(2)}) async-start(s32[32,1,2]{2,1,0:T(1,128)} %bitcast.1), calls=%async_computation | async-start | bytes 32768 | tf_op jit(solution)/shard_map/all_to_all | solution.py:141
  24.2 1.3 reshape.132
  26.1 1.3 reshape.133
  27.4 6.1 %all-to-all-done = s32[32,1,2]{2,1,0:T(1,128)S(1)} async-done(((s32[32,1,2]{2,1,0:T(1,128)}), s32[32,1,2]{2,1,0:T(1,128)S(1)}, u32[]{:S(2)}, u32[]{:S(2)}) %all-to-all-start) | async-done | bytes 288 | tf_op jit(solution)/shard_map/all_to_all | solution.py:141
  33.5 4.4 all-to-all-start.1
  38.9 18.5 %all-gather.3.cloned.1.call-done = bf16[1024,512]{1,0:T(8,128)(2,1)} async-done(((bf16[128,512]{1,0:T(8,128)(2,1)}), bf16[1024,512]{1,0:T(8,128)(2,1)}) %all-gather.3.cloned.1.call-update) | async-done | bytes 1048592 | tf_op jit(solution)/shard_map/all_gather | solution.py:58
  57.4 8.4 %all-to-all-done.1 = bf16[32,16,1024]{2,1,0:T(8,128)(2,1)S(1)} async-done(((bf16[32,16,1024]{2,1,0:T(8,128)(2,1)}), bf16[32,16,1024]{2,1,0:T(8,128)(2,1)S(1)}, u32[]{:S(2)}, u32[]{:S(2)}) %all-to-all-start.1) | async-done | bytes 1048608 | tf_op jit(solution)/shard_map/all_to_all | solution.py:134
  65.8 2.4 fusion.20
  68.4 3.5 fusion.18
  72.0 43.9 %all-gather.5.cloned.1.call-done = bf16[512,1920]{1,0:T(8,128)(2,1)} async-done(((bf16[64,1920]{1,0:T(8,128)(2,1)}), bf16[512,1920]{1,0:T(8,128)(2,1)}) %all-gather.5.cloned.1.call-update) | async-done | bytes 1966096 | tf_op jit(solution)/shard_map/all_gather | solution.py:66
  115.8 4.4 fusion.21
  120.2 1.6 copy.33
  123.1 1.3 multiply_reduce_fusion.1
  125.6 2.1 fusion.7
  128.4 4.9 fusion.15
  134.6 2.1 fusion.8
  136.6 10.4 %all-to-all-start.2 = ((f32[32,16,1024]{2,1,0:T(8,128)}), f32[32,16,1024]{2,1,0:T(8,128)}, u32[]{:S(2)}, u32[]{:S(2)}) async-start(f32[32,16,1024]{2,1,0:T(8,128)} %bitcast.18), calls=%async_computation.2 | async-start | bytes 4194304 | tf_op jit(solution)/shard_map/all_to_all | solution.py:154
  147.7 92.0 %all-reduce = (f32[4,512]{1,0:T(4,128)S(1)}, f32[1920]{0:T(1024)S(1)}) all-reduce(f32[4,512]{1,0:T(4,128)S(1)} %pad_maximum_fusion, f32[1920]{0:T(1024)S(1)} %convert_reduce_fusion), channel_id=1, replica_groups=mesh['dp'=32,'param'=8] {'dp','param'}, use_global_device_ids=true, to_apply=%region_19.20 | all-reduce | flops 3968 | bytes 31744 | tf_op jit(solution)/shard_map/psum | solution.py:91
  240.3 57.1 %reduce-scatter.5.cloned.1.call-done = f32[64,1920]{1,0:T(8,128)} async-done(((f32[512,1920]{1,0:T(8,128)}), f32[64,1920]{1,0:T(8,128)}) %reduce-scatter.5.cloned.1.call-update) | async-done | bytes 491536 | tf_op jit(solution)/shard_map/reduce_scatter | solution.py:77
  298.0 4.9 add_select_fusion
  302.9 1.7 reshape.136
  306.8 257.3 %all-reduce.4.cloned.1.call-done = (f32[128,512]{1,0:T(8,128)}, f32[64,1920]{1,0:T(8,128)}) async-done(((f32[128,512]{1,0:T(8,128)}, f32[64,1920]{1,0:T(8,128)}), (f32[128,512]{1,0:T(8,128)}, f32[64,1920]{1,0:T(8,128)})) %all-reduce.4.cloned.1.call-update) | async-done | bytes 753680 | tf_op jit(solution)/shard_map/psum | solution.py:90
  564.1 1.7 broadcast_multiply_fusion.1
  565.7 1.8 broadcast_multiply_fusion
  (58 shorter events, 14.5 us)
Async XLA Ops:
  7.2 50.2 %all-gather.3.cloned.1.call-start = ((), (), s32[]{:S(2)}) async-start(), calls=%async_computation.5 | async-start | bytes 1179648 | tf_op jit(solution)/shard_map/all_gather | solution.py:58
  11.6 21.9 %all-to-all-start = ((s32[32,1,2]{2,1,0:T(1,128)}), s32[32,1,2]{2,1,0:T(1,128)S(1)}, u32[]{:S(2)}, u32[]{:S(2)}) async-start(s32[32,1,2]{2,1,0:T(1,128)} %bitcast.1), calls=%async_computation | async-start | bytes 32768 | tf_op jit(solution)/shard_map/all_to_all | solution.py:141
  33.5 32.3 %all-to-all-start.1 = ((bf16[32,16,1024]{2,1,0:T(8,128)(2,1)}), bf16[32,16,1024]{2,1,0:T(8,128)(2,1)S(1)}, u32[]{:S(2)}, u32[]{:S(2)}) async-start(bf16[32,16,1024]{2,1,0:T(8,128)(2,1)} %reshape.133), calls=%async_computation.1 | async-start | bytes 2097152 | tf_op jit(solution)/shard_map/all_to_all | solution.py:134
  37.9 77.9 %all-gather.5.cloned.1.call-start = ((), (), s32[]{:S(2)}) async-start(), calls=%async_computation.6 | async-start | bytes 2211840 | tf_op jit(solution)/shard_map/all_gather | solution.py:66
  38.6 201.7 %reduce-scatter.3.cloned.1.call-start = ((), (), s32[]{:S(2)}) async-start(), calls=%async_computation.7 | async-start | bytes 2359296 | tf_op jit(solution)/shard_map/reduce_scatter | solution.py:84
  65.8 2.6 copy-start.1
  65.8 2.6 copy-start.5
  65.8 2.6 copy-start.7
  120.2 1.6 copy-start.6
  121.8 1.2 copy-start
  124.4 1.2 copy-start.2
  127.7 0.7 copy-start.9
  127.8 169.6 %reduce-scatter.5.cloned.1.call-start = ((), (), s32[]{:S(2)}) async-start(), calls=%async_computation.8 | async-start | bytes 4423680 | tf_op jit(solution)/shard_map/reduce_scatter | solution.py:77
  133.3 1.2 copy-start.4
  136.6 10.6 %copy-start.3 = (bf16[512,1920]{1,0:T(8,128)(2,1)S(1)}, bf16[512,1920]{1,0:T(8,128)(2,1)}, u32[]{:S(2)}) copy-start(bf16[512,1920]{1,0:T(8,128)(2,1)} %param.21) | copy-start | bytes 5898244
  136.6 166.3 %all-to-all-start.2 = ((f32[32,16,1024]{2,1,0:T(8,128)}), f32[32,16,1024]{2,1,0:T(8,128)}, u32[]{:S(2)}, u32[]{:S(2)}) async-start(f32[32,16,1024]{2,1,0:T(8,128)} %bitcast.18), calls=%async_computation.2 | async-start | bytes 4194304 | tf_op jit(solution)/shard_map/all_to_all | solution.py:154
  147.0 151.0 %copy-start.8 = (f32[1920]{0:T(1024)S(1)}, f32[1920]{0:T(1024)}, u32[]{:S(2)}) copy-start(f32[1920]{0:T(1024)} %param.20) | copy-start | bytes 23044
  147.0 417.1 %all-reduce.4.cloned.1.call-start = ((), (), s32[]{:S(2)}) async-start(), calls=%async_computation.9 | async-start | bytes 1507328 | tf_op jit(solution)/shard_map/psum | solution.py:90
Sparse Core Ops, SparseCore 0:
  9.8 47.5 all-gather.2
  59.2 56.6 all-gather.4
  127.9 77.3 reduce-scatter.2
  208.3 89.0 reduce-scatter.4
  299.9 264.0 all-reduce.3
where the time goes:
time: 577 us; the launch traced here: 574 us
  waiting for transfers between devices  393 us (68%)
  blocking collectives  92 us (16%)
  starting transfers between devices  27.7 us (5%)
  matrix products  22.3 us (4%)
  other arithmetic  14.4 us (2%)
  between operations  14 us (2%)
  local copies, waits for them, and re-layouts  11.1 us (2%)
    psum x1, waiting for transfers between devices, project_backward(): replica = lax.psum((conv_grad, proj_grad), 'dp')  257 us
    psum x1, blocking collectives, project_backward(): shared = lax.psum((norm_local, bias_local), ('dp', 'param'))  92 us
    reduce_scatter x1, waiting for transfers between devices, project_backward(): lax.psum_scatter(contract_rows(window, upstream), 'param', scatter_dimens...  57.1 us
    all_gather x1, waiting for transfers between devices, project_forward(): lax.all_gather(proj_weight, 'param', axis=0, tiled=True)  43.9 us
    all_gather x1, waiting for transfers between devices, project_forward(): lax.all_gather(conv_weight, 'param', axis=0, tiled=True)  18.5 us
    all_to_all x1, starting transfers between devices, on_device(): lax.all_to_all(slot_live, 'dp', split_axis=0, concat_axis=0, tiled=True)  12.6 us
  transfers between devices with their start and end apart: 8, of which 6 were waited for; matrix products, arithmetic and copies ran while one was open for 5% of the time, Pallas kernels for 0%

commit v1 on v0

v1 whole, which is shorter than its diff:
```python
import functools
import math

import jax
import jax.numpy as jnp
from jax import lax
from jax.experimental import pallas as pl
from jax.experimental.pallas import tpu as pltpu
from jax.sharding import PartitionSpec as P

CAP = 2
SEG = 8
MARK = 64.0
MESH = pl.DeviceIdType.MESH
VMEM = pltpu.VMEM

epsilon = 1e-05


def normalize(values, factor, offset):
    average = jnp.mean(values, axis=-1, keepdims=True)
    centred = values - average
    spread = jnp.mean(centred * centred, axis=-1, keepdims=True)
    return centred * lax.rsqrt(spread + epsilon) * factor + offset


def encode_tail(hidden, conv_gain, conv_shift, feat_gain, feat_shift):
    active = jax.nn.gelu(normalize(hidden, conv_gain, conv_shift), approximate=False)
    return normalize(active, feat_gain, feat_shift)


def contract_rows(left, right):
    return lax.dot_general(
        left, right, (((0,), (0,)), ((), ())), preferred_element_type=jnp.float32
    )


def contract_cols(left, right):
    return lax.dot_general(
        left, right, (((1,), (1,)), ((), ())), preferred_element_type=jnp.float32
    )


def remote(src, dst, send, recv, device):
    return pltpu.make_async_remote_copy(
        src_ref=src,
        dst_ref=dst,
        send_sem=send,
        recv_sem=recv,
        device_id=device,
        device_id_type=MESH,
    )


def loop(first, last, body):
    def step(index, carry):
        body(index)
        return carry

    lax.fori_loop(first, last, step, 0)


def greet(me_dp, me_par, n_dp, n_par):
    barrier = pltpu.get_barrier_semaphore()

    def over_dp(k):
        pl.semaphore_signal(
            barrier, inc=1, device_id=(lax.rem(me_dp + k, n_dp), me_par), device_id_type=MESH
        )

    def over_par(k):
        pl.semaphore_signal(
            barrier, inc=1, device_id=(me_dp, lax.rem(me_par + k, n_par)), device_id_type=MESH
        )

    loop(1, n_dp, over_dp)
    loop(1, n_par, over_par)
    pl.semaphore_wait(barrier, n_dp + n_par - 2)


def slot_targets(dest, live, frames, segments):
    seg = lax.broadcasted_iota(jnp.int32, (segments, frames), 0)
    frame = lax.broadcasted_iota(jnp.int32, (segments, frames), 1)
    owner = frame // SEG
    mine = owner == seg
    dest_all = jnp.broadcast_to(dest, (segments, frames)).astype(jnp.float32)
    live_all = jnp.broadcast_to(live, (segments, frames)).astype(jnp.float32)
    dest_row = jnp.sum(jnp.where(mine, dest_all, 0.0), axis=0, keepdims=True)
    live_row = jnp.sum(jnp.where(mine, live_all, 0.0), axis=0, keepdims=True)
    same = jnp.where(dest_all == dest_row, 1.0, 0.0)
    rank = jnp.sum(jnp.where(seg < owner, same, 0.0), axis=0, keepdims=True)
    position = (lax.broadcasted_iota(jnp.int32, (1, frames), 1) % SEG).astype(jnp.float32)
    row = (dest_row * CAP + rank) * SEG + position
    return jnp.where(position < live_row, row, -1.0)


def deliver_kernel(
    n_dp,
    n_par,
    conv_ref,
    dest_ref,
    live_ref,
    wc_ref,
    wp_ref,
    x_ref,
    wc_full,
    wp_full,
    place_ref,
    packed,
    x_send,
    x_recv,
    w_send,
    w_recv,
    f_send,
    f_recv,
):
    me_dp, me_par = lax.axis_index("dp"), lax.axis_index("param")
    core = lax.rem(me_dp, 2)
    mate = me_dp + 1 - 2 * core
    unit = CAP * SEG
    frames = conv_ref.shape[0]
    weights = ((wc_ref, wc_full), (wp_ref, wp_full))
    greet(me_dp, me_par, n_dp, n_par)

    def half_rows(ref, owner, which):
        rows = ref.shape[0]
        half = rows // 2
        return pl.ds(pl.multiple_of(owner * rows + which * half, half), half)

    def send_weight(w, k, shard, full):
        half = shard.shape[0] // 2
        return remote(
            shard.at[pl.ds(pl.multiple_of(core * half, half), half)],
            full.at[half_rows(shard, me_par, core)],
            w_send.at[w, k],
            w_recv.at[w, k],
            (me_dp, lax.rem(me_par + k, n_par)),
        )

    def pass_on(w, k, shard, full, which):
        rows = full.at[half_rows(shard, lax.rem(me_par + n_par - k, n_par), which)]
        return remote(rows, rows, f_send.at[w, k], f_recv.at[w, k], (mate, me_par))

    for w, (shard, full) in enumerate(weights):
        loop(1, n_par, lambda k: send_weight(w, k, shard, full).start())

    target = slot_targets(dest_ref[...], live_ref[...], frames, frames // SEG)
    block = 128

    def pack(t):
        rows = pl.ds(pl.multiple_of(t * block, block), block)
        here = (lax.broadcasted_iota(jnp.int32, (block, frames), 0) + t * block).astype(jnp.float32)
        hit = jnp.where(here == target, 1.0, 0.0)
        empty = 1.0 - jnp.sum(hit, axis=1, keepdims=True)
        place = hit.astype(jnp.bfloat16)
        place_ref[rows, :] = place
        moved = jnp.dot(place, conv_ref[...], preferred_element_type=jnp.float32)
        packed[rows, :] = (moved + empty * MARK).astype(jnp.bfloat16)

    loop(0, n_dp * unit // block, pack)

    def own_rows(index):
        return pl.ds(pl.multiple_of(index * unit, unit), unit)

    def send_rows(k):
        to = lax.rem(me_dp + k, n_dp)
        return remote(
            packed.at[own_rows(to)],
            x_ref.at[own_rows(me_dp)],
            x_send.at[k],
            x_recv.at[k],
            (to, me_par),
        )

    def recv_rows(k):
        source = lax.rem(me_dp + n_dp - k, n_dp)
        rows = x_ref.at[own_rows(source)]
        return remote(rows, rows, x_send.at[k], x_recv.at[k], (source, me_par))

    loop(1, n_dp, lambda k: send_rows(k).start())
    x_ref[own_rows(me_dp), :] = packed[own_rows(me_dp), :]
    for shard, full in weights:
        rows = shard.shape[0]
        full[pl.ds(pl.multiple_of(me_par * rows, rows), rows), :] = shard[...]

    for w, (shard, full) in enumerate(weights):

        def relay(k):
            rows = full.at[half_rows(shard, lax.rem(me_par + n_par - k, n_par), core)]
            remote(rows, rows, w_send.at[w, k], w_recv.at[w, k], (mate, me_par)).wait_recv()
            pass_on(w, k, shard, full, core).start()

        loop(1, n_par, relay)
    for w, (shard, full) in enumerate(weights):

        def settle(k):
            pass_on(w, k, shard, full, 1 - core).wait_recv()
            pass_on(w, k, shard, full, core).wait_send()
            send_weight(w, k, shard, full).wait_send()

        loop(1, n_par, settle)

    def finish(k):
        recv_rows(k).wait_recv()
        send_rows(k).wait_send()

    loop(1, n_dp, finish)


def deliver(conv_input, dest, live, conv_weight, proj_weight, n_dp, n_par):
    frames, width = conv_input.shape
    slots = n_dp * CAP * SEG
    whole = pl.BlockSpec(memory_space=VMEM)
    dma = pltpu.SemaphoreType.DMA
    return pl.pallas_call(
        functools.partial(deliver_kernel, n_dp, n_par),
        out_shape=(
            jax.ShapeDtypeStruct((slots, width), jnp.bfloat16),
            jax.ShapeDtypeStruct((conv_weight.shape[0] * n_par, conv_weight.shape[1]), jnp.bfloat16),
            jax.ShapeDtypeStruct((proj_weight.shape[0] * n_par, proj_weight.shape[1]), jnp.bfloat16),
            jax.ShapeDtypeStruct((slots, frames), jnp.bfloat16),
        ),
        in_specs=[whole] * 5,
        out_specs=(whole,) * 4,
        scratch_shapes=[
            pltpu.VMEM((slots, width), jnp.bfloat16),
            dma((n_dp,)),
            dma((n_dp,)),
            dma((2, n_par)),
            dma((2, n_par)),
            dma((2, n_par)),
            dma((2, n_par)),
        ],
        compiler_params=pltpu.CompilerParams(
            collective_id=0, has_side_effects=True, vmem_limit_bytes=32 * 1024 * 1024
        ),
        name="deliver",
    )(conv_input, dest, live, conv_weight, proj_weight)


def piece_grid(n_chip):
    side = math.isqrt(n_chip)
    return side, n_chip // side


def reduce_kernel(
    n_dp,
    n_par,
    scale,
    back_ref,
    gc_ref,
    gp_ref,
    gs_ref,
    ret_ref,
    oc_ref,
    op_ref,
    os_ref,
    c0c,
    c0p,
    s1c,
    s1p,
    r1c,
    r1p,
    r1s,
    s2c,
    s2p,
    s2s,
    r2c,
    r2p,
    r2s,
    b_send,
    b_recv,
    m_send,
    m_recv,
    p_send,
    p_recv,
    d_send,
    d_recv,
    e_send,
    e_recv,
    g_send,
    g_recv,
    h_send,
    h_recv,
    k_send,
    k_recv,
):
    me_dp, me_par = lax.axis_index("dp"), lax.axis_index("param")
    core = lax.rem(me_dp, 2)
    mate = me_dp + 1 - 2 * core
    n_chip = n_dp // 2
    me_chip = me_dp // 2
    unit = CAP * SEG
    greet(me_dp, me_par, n_dp, n_par)

    def own_rows(index):
        return pl.ds(pl.multiple_of(index * unit, unit), unit)

    def back_rows(k):
        to = lax.rem(me_dp + k, n_dp)
        return remote(
            back_ref.at[own_rows(to)],
            ret_ref.at[own_rows(me_dp)],
            b_send.at[k],
            b_recv.at[k],
            (to, me_par),
        )

    def back_wait(k):
        source = lax.rem(me_dp + n_dp - k, n_dp)
        rows = ret_ref.at[own_rows(source)]
        remote(rows, rows, b_send.at[k], b_recv.at[k], (source, me_par)).wait_recv()
        back_rows(k).wait_send()

    def par_at(k):
        return lax.rem(me_par + k, n_par)

    def from_par(k):
        return lax.rem(me_par + n_par - k, n_par)

    def halves(ref, which):
        half = ref.shape[1] // 2
        return pl.ds(pl.multiple_of(which * half, half), half)

    mates = ((gc_ref, c0c), (gp_ref, c0p))

    def to_mate(w, k):
        grad, landing = mates[w]
        block = par_at(k)
        return remote(
            grad.at[block, halves(grad, 1 - core)],
            landing.at[block],
            m_send.at[w, k],
            m_recv.at[w, k],
            (mate, me_par),
        )

    def start_mate(k):
        to_mate(0, k).start()
        to_mate(1, k).start()

    loop(1, n_par, start_mate)
    start_mate(0)

    def small_out(k):
        return remote(
            gs_ref.at[par_at(k)],
            r1s.at[k],
            p_send.at[2, k],
            p_recv.at[2, k],
            (me_dp, par_at(k)),
        )

    loop(1, n_par, lambda k: small_out(k).start())
    loop(1, n_dp, lambda k: back_rows(k).start())
    ret_ref[own_rows(me_dp), :] = back_ref[own_rows(me_dp), :]

    stages = ((s1c, r1c), (s1p, r1p))

    def to_par(w, k):
        sent, landing = stages[w]
        return remote(
            sent.at[k], landing.at[k], p_send.at[w, k], p_recv.at[w, k], (me_dp, par_at(k))
        )

    def summed(w, k):
        grad, landing = mates[w]
        to_mate(w, k).wait_recv()
        block = par_at(k)
        return grad[block, halves(grad, core), :] + landing[block]

    def pair_sum(k):
        for w in range(2):
            stages[w][0][k] = summed(w, k).astype(jnp.bfloat16)
            to_par(w, k).start()

    loop(1, n_par, pair_sum)
    s2c[...] = summed(0, 0)
    width = gp_ref.shape[2]
    s2p[:, width:] = jnp.zeros((s2p.shape[0], s2p.shape[1] - width), jnp.float32)
    s2p[:, :width] = summed(1, 0)
    s2s[...] = gs_ref[me_par]

    def gather_par(k):
        for w in range(2):
            to_par(w, k).wait_recv()
        small_out(k).wait_recv()
        s2c[...] += r1c[k].astype(jnp.float32)
        s2p[:, :width] += r1p[k].astype(jnp.float32)
        s2s[...] += r1s[k]

    loop(1, n_par, gather_par)

    rows_n, cols_n = piece_grid(n_chip)

    def region(shape, chip, top):
        tall, wide = shape[0] // rows_n, shape[1] // cols_n
        row, col = chip // cols_n, lax.rem(chip, cols_n)
        return (
            pl.ds(pl.multiple_of(top + row * tall, tall), tall),
            pl.ds(pl.multiple_of(col * wide, wide), wide),
        )

    def chip_at(k):
        return lax.rem(me_chip + k, n_chip)

    def chip_from(k):
        return lax.rem(me_chip + n_chip - k, n_chip)

    spread = ((s2c, r2c, oc_ref), (s2p, r2p, op_ref))

    def to_chip(w, k):
        held, landing, _ = spread[w]
        to = chip_at(k)
        return remote(
            held.at[region(held.shape, to, 0)],
            landing.at[k],
            d_send.at[w, k],
            d_recv.at[w, k],
            (to * 2 + core, me_par),
        )

    def start_chip(k):
        to_chip(0, k).start()
        to_chip(1, k).start()

    def small_dp(k):
        to = lax.rem(me_dp + k, n_dp)
        return remote(s2s, r2s.at[k], e_send.at[k], e_recv.at[k], (to, me_par))

    loop(1, n_chip, start_chip)
    loop(1, n_dp, lambda k: small_dp(k).start())

    def final_region(w, chip, which):
        held = spread[w][0]
        return region(held.shape, chip, which * held.shape[0])

    def from_chip(k):
        for w in range(2):
            to_chip(w, k).wait_recv()
            out = spread[w][2]
            out[final_region(w, me_chip, core)] += spread[w][1][k]

    for w in range(2):
        held, _, out = spread[w]
        out[final_region(w, me_chip, core)] = held[region(held.shape, me_chip, 0)]
    loop(1, n_chip, from_chip)
    for w in range(2):
        out = spread[w][2]
        out[final_region(w, me_chip, core)] = out[final_region(w, me_chip, core)] * scale

    def share(w, k):
        out = spread[w][2]
        rows = out.at[final_region(w, me_chip, core)]
        return remote(rows, rows, g_send.at[w, k], g_recv.at[w, k], (chip_at(k) * 2 + core, me_par))

    def share_wait(w, k):
        out = spread[w][2]
        rows = out.at[final_region(w, chip_from(k), core)]
        remote(
            rows, rows, g_send.at[w, k], g_recv.at[w, k], (chip_from(k) * 2 + core, me_par)
        ).wait_recv()

    def start_share(k):
        share(0, k).start()
        share(1, k).start()

    loop(1, n_chip, start_share)

    total = s2s[...]
    os_ref[me_par] = total

    def small_sum(k):
        small_dp(k).wait_recv()
        os_ref[me_par] += r2s[k]

    loop(1, n_dp, small_sum)
    os_ref[me_par] = os_ref[me_par] * scale

    def small_share(k, owner, to):
        rows = os_ref.at[owner]
        return remote(rows, rows, h_send.at[k], h_recv.at[k], (me_dp, to))

    loop(1, n_par, lambda k: small_share(k, me_par, par_at(k)).start())

    def end_share(k):
        share_wait(0, k)
        share_wait(1, k)

    loop(1, n_chip, end_share)

    def to_core(w, which):
        out = spread[w][2]
        half = out.shape[0] // 2
        rows = out.at[pl.ds(pl.multiple_of(which * half, half), half)]
        return remote(rows, rows, k_send.at[w], k_recv.at[w], (mate, me_par))

    for w in range(2):
        to_core(w, core).start()

    loop(1, n_dp, back_wait)

    def par_end(k):
        small_share(k, from_par(k), from_par(k)).wait_recv()
        small_share(k, me_par, par_at(k)).wait_send()
        small_out(k).wait_send()
        for w in range(2):
            to_par(w, k).wait_send()

    loop(1, n_par, par_end)

    def mate_end(k):
        for w in range(2):
            to_mate(w, k).wait_send()

    loop(0, n_par, mate_end)

    def chip_end(k):
        for w in range(2):
            to_chip(w, k).wait_send()
            share(w, k).wait_send()

    loop(1, n_chip, chip_end)
    loop(1, n_dp, lambda k: small_dp(k).wait_send())
    for w in range(2):
        to_core(w, 1 - core).wait_recv()
        to_core(w, core).wait_send()


def reduce_all(back, conv_grad, proj_grad, small, n_dp, n_par, scale):
    n_chip = n_dp // 2
    _, conv_rows, conv_cols = conv_grad.shape
    _, proj_rows, proj_cols = proj_grad.shape
    rows_n, cols_n = piece_grid(n_chip)
    wide = -(-proj_cols // (128 * cols_n)) * 128 * cols_n
    hc, hp = conv_rows // 2, proj_rows // 2
    tile = small.shape[1:]
    f32, b16 = jnp.float32, jnp.bfloat16
    whole = pl.BlockSpec(memory_space=VMEM)
    dma = pltpu.SemaphoreType.DMA
    return pl.pallas_call(
        functools.partial(reduce_kernel, n_dp, n_par, scale),
        out_shape=(
            jax.ShapeDtypeStruct(back.shape, b16),
            jax.ShapeDtypeStruct((conv_rows, conv_cols), f32),
            jax.ShapeDtypeStruct((proj_rows, wide), f32),
            jax.ShapeDtypeStruct(small.shape, f32),
        ),
        in_specs=[whole] * 4,
        out_specs=(whole,) * 4,
        scratch_shapes=[
            pltpu.VMEM((n_par, hc, conv_cols), f32),
            pltpu.VMEM((n_par, hp, proj_cols), f32),
            pltpu.VMEM((n_par, hc, conv_cols), b16),
            pltpu.VMEM((n_par, hp, proj_cols), b16),
            pltpu.VMEM((n_par, hc, conv_cols), b16),
            pltpu.VMEM((n_par, hp, proj_cols), b16),
            pltpu.VMEM((n_par,) + tile, f32),
            pltpu.VMEM((hc, conv_cols), f32),
            pltpu.VMEM((hp, wide), f32),
            pltpu.VMEM(tile, f32),
            pltpu.VMEM((n_chip, hc // rows_n, conv_cols // cols_n), f32),
            pltpu.VMEM((n_chip, hp // rows_n, wide // cols_n), f32),
            pltpu.VMEM((n_dp,) + tile, f32),
            dma((n_dp,)),
            dma((n_dp,)),
            dma((2, n_par)),
            dma((2, n_par)),
            dma((3, n_par)),
            dma((3, n_par)),
            dma((2, n_chip)),
            dma((2, n_chip)),
            dma((n_dp,)),
            dma((n_dp,)),
            dma((2, n_chip)),
            dma((2, n_chip)),
            dma((n_par,)),
            dma((n_par,)),
            dma((2,)),
            dma((2,)),
        ],
        compiler_params=pltpu.CompilerParams(
            collective_id=1, has_side_effects=True, vmem_limit_bytes=48 * 1024 * 1024
        ),
        name="reduce_all",
    )(back, conv_grad, proj_grad, small)


def on_device(
    conv_input,
    block_dest,
    live_frames,
    conv_weight,
    conv_gain,
    conv_shift,
    feat_gain,
    feat_shift,
    proj_weight,
    proj_bias,
    cotangent,
):
    n_dp = lax.axis_size("dp")
    n_par = lax.axis_size("param")
    frames_dev = conv_input.shape[0]
    grad_scale = 1.0 / math.sqrt(frames_dev * n_dp * n_par)
    arrived, conv_full, proj_full, place = deliver(
        conv_input, block_dest, live_frames[:, None], conv_weight, proj_weight, n_dp, n_par
    )
    live = arrived[:, :1] < MARK / 2
    rows = jnp.where(live, arrived, jnp.zeros_like(arrived))
    upstream = jnp.where(live, cotangent, jnp.zeros_like(cotangent))
    hidden = jnp.dot(rows, conv_full, preferred_element_type=jnp.float32)
    tail_out, pullback = jax.vjp(
        encode_tail, hidden, conv_gain, conv_shift, feat_gain, feat_shift
    )
    features = tail_out.astype(jnp.bfloat16)
    lifted = jnp.dot(features, proj_full, preferred_element_type=jnp.float32)
    projected = jnp.where(live, lifted + proj_bias, 0.0)
    proj_grad = contract_rows(features, upstream)
    back_feat = contract_cols(upstream, proj_full)
    grads = pullback(back_feat)
    hidden_back = grads[0].astype(jnp.bfloat16)
    conv_grad = contract_rows(rows, hidden_back)
    channels = conv_gain.shape[0]
    model = proj_bias.shape[0]
    bias_local = jnp.sum(upstream, axis=0, dtype=jnp.float32)
    small = jnp.concatenate([grads[1], grads[2], grads[3], grads[4], bias_local])
    small = jnp.pad(small, (0, n_par * 1024 - small.shape[0])).reshape(n_par, 8, 128)
    returned, conv_out, proj_out, small_out = reduce_all(
        hidden_back,
        conv_grad.reshape(n_par, -1, channels),
        proj_grad.reshape(n_par, -1, model),
        small,
        n_dp,
        n_par,
        grad_scale,
    )
    mine = contract_rows(place, returned).astype(jnp.bfloat16)
    frames_grad = contract_cols(mine, conv_full)
    flat = small_out.reshape(-1)
    return (
        projected,
        frames_grad,
        conv_out,
        proj_out[:, :model],
        flat[: 4 * channels].reshape(4, channels),
        flat[4 * channels : 4 * channels + model],
    )


def solution(mesh):
    return jax.shard_map(
        on_device,
        mesh=mesh,
        in_specs=(
            P(("dp", "param"), None),
            P(("dp", "param"), None),
            P(("dp", "param")),
            P("param", None),
            P(),
            P(),
            P(),
            P(),
            P("param", None),
            P(),
            P(("dp", "param"), None),
        ),
        out_specs=(
            P(("dp", "param"), None),
            P(("dp", "param"), None),
            P("param", None),
            P("param", None),
            P(),
            P(),
        ),
        check_vma=False,
    )
```

time: 577 us -> 137 us (0.24)
  waiting for transfers between devices: 393 us -> 0 us
  Pallas kernels: 0 us -> 102 us
  blocking collectives: 92 us -> 0 us
  starting transfers between devices: 27.7 us -> 0 us
  between operations: 14 us -> 0.88 us
  matrix products: 22.3 us -> 15.9 us
    psum x1 -> x0, waiting for transfers between devices: 257 us -> none  [project_backward(): replica = lax.psum((conv_grad, proj_grad), 'dp')]
    pallas_call x0 -> x2, Pallas kernels: none -> 102 us  [the longest x1 60 us: reduce_all(): pl.pallas_call(functools.partial(reduce_kernel, n_dp, n_par, scale), out_...]
    psum x1 -> x0, blocking collectives: 92 us -> none  [project_backward(): shared = lax.psum((norm_local, bias_local), ('dp', 'param'))]
    all_gather x2 -> x0, waiting for transfers between devices: 62.3 us -> none  [the longest x1 43.9 us: project_forward(): lax.all_gather(proj_weight, 'param', axis=0, tiled=True)]
    reduce_scatter x2 -> x0, waiting for transfers between devices: 57.1 us -> none  [the longest x1 57.1 us: project_backward(): lax.psum_scatter(contract_rows(window, upstream), 'param', scatter_dimens...]
    all_to_all x3 -> x0, starting transfers between devices: 27.3 us -> none  [the longest x1 12.6 us: on_device(): lax.all_to_all(slot_live, 'dp', split_axis=0, concat_axis=0, tiled=True)]
    all_to_all x3 -> x0, waiting for transfers between devices: 14.5 us -> none  [the longest x1 8.41 us: on_device(): lax.all_to_all(sending.reshape(dp_count, CAP * segment, in_width), 'dp',...]
  transfers between devices with their start and end apart: 8 -> 0, of which waited for: 6 -> 0; matrix products, arithmetic and copies ran while one was open for 5% -> 0% of each run, Pallas kernels for 0% -> 0%
where the time goes in v1:
time: 137 us
  Pallas kernels  102 us (74%)
  matrix products  15.9 us (12%)
  other arithmetic  8.76 us (6%)
  local copies, waits for them, and re-layouts  8.74 us (6%)
    pallas_call x1, Pallas kernels, reduce_all(): pl.pallas_call(functools.partial(reduce_kernel, n_dp, n_par, scale), out_...  60 us
    pallas_call x1, Pallas kernels, deliver(): pl.pallas_call(functools.partial(deliver_kernel, n_dp, n_par), out_shape=...  42.2 us
    dot_general x2, matrix products, contract_rows(): lax.dot_general(left, right, (((0,), (0,)), ((), ())), preferred_element_...  5.87 us
    dot_general x1, matrix products, on_device(): lifted = jnp.dot(features, proj_full, preferred_element_type=jnp.float32)  5.11 us
    unnamed x33, local copies, waits for them, and re-layouts  4.39 us
    dot_general x2, matrix products, contract_cols(): lax.dot_general(left, right, (((1,), (1,)), ((), ())), preferred_element_...  3.13 us
    reduce_sum x1, other arithmetic, normalize(): average = jnp.mean(values, axis=-1, keepdims=True)  2.91 us

profile of v1, /device:TPU:1, one launch (start us, length us, event | category | flops | bytes accessed | tf_op | source)
XLA Modules:
  0.0 136.5 jit_solution(15883437526580123856)
XLA Ops:
  0.6 0.7 copy.20.dest_ref
  1.4 0.7 copy.21.live_ref
  2.1 1.0 copy-done
  3.1 0.9 copy-done.1
  4.1 0.9 copy-done.2
  5.0 42.2 %deliver.1 = (bf16[512,1024]{1,0:T(8,128)(2,1)S(1)}, bf16[1024,512]{1,0:T(8,128)(2,1)S(1)}, bf16[512,1920]{1,0:T(8,128)(2,1)S(1)}, bf16[512,256]{1,0:T(8,128)(2,1)S(1)}) custom-call(bf16[256,1024]{1,0:T(8,128)(2,1)S(1)} %copy-done, s32[32,1]{1,0:T(8,128)S(1)} %copy.20.dest_ref, s32[32,1]{1,0:T(8,128)S(1)} %copy.21.live_ref, bf16[128,512]{1,0:T(8,128)(2,1)S(1)} %copy-done.2, ...), custom_call_target="tpu_custom_call" | custom-call | tf_op jit(solution)/shard_map/deliver/pallas_call | solution.py:215
  47.4 1.8 %fusion.19 = (f32[512]{0:T(512)S(1)}, f32[512,512]{0,1:T(8,128)}) fusion(bf16[1024,512]{1,0:T(8,128)(2,1)S(1)} %get-tuple-element.15, bf16[512,1024]{1,0:T(8,128)(2,1)S(1)} %get-tuple-element.14, pred[512]{0:T(512)(128)(4,1)S(1)} %compare_reduce_fusion), kind=kOutput, calls=%fused_computation.60 | convolution fusion | flops 537656832 | bytes 3148288 | tf_op jit(solution)/shard_map/dot_general | solution.py:612
  49.2 1.6 %copy.22 = f32[512,512]{1,0:T(8,128)S(1)} copy(f32[512,512]{0,1:T(8,128)} %get-tuple-element.39) | data formatting | bytes 2097152 | tf_op jit(solution)/shard_map/dot_general | solution.py:612
  50.9 0.3 multiply_reduce_fusion.5
  51.2 2.9 %fusion.17 = (f32[512]{0:T(512)S(1)}, f32[512,512]{1,0:T(8,128)S(1)}, f32[512,512]{1,0:T(8,128)S(1)}) fusion(f32[512]{0:T(512)S(1)} %copy-done.10, f32[512]{0:T(512)S(1)} %copy-done.9, f32[512]{0:T(512)S(1)} %fusion.10, f32[512,512]{1,0:T(8,128)S(1)} %copy.22, f32[512]{0:T(512)S(1)} %broadcast_multiply_fusion.1), kind=kLoop, calls=%fused_computation.59 | loop fusion | flops 18087424 | bytes 3155968 | tf_op jit(solution)/shard_map/jvp()/reduce_sum | solution.py:21
  54.1 1.5 %multiply_reduce_fusion.3 = (f32[512]{0:T(512)S(1)}, f32[512]{0:T(512)S(1)}, f32[512]{0:T(512)S(1)}, f32[512,512]{1,0:T(8,128)S(1)}) fusion(f32[512,512]{1,0:T(8,128)S(1)} %get-tuple-element.34, f32[512]{0:T(512)S(1)} %copy-done.11, f32[512]{0:T(512)S(1)} %broadcast_multiply_fusion, bf16[512,1920]{1,0:T(8,128)(2,1)S(1)} %copy-done.4, ...), kind=kOutput, calls=%fused_computation.14 | convolution fusion | flops 1009449472 | bytes 6040064 | tf_op jit(solution)/shard_map/dot_general | solution.py:39
  55.6 0.6 multiply_reduce_fusion
  56.2 2.2 %multiply_reduce_fusion.1 = (f32[512]{0:T(512)S(1)}, f32[512]{0:T(512)S(1)}, f32[512]{0:T(512)S(1)}, f32[512,512]{1,0:T(8,128)}) fusion(f32[512,512]{1,0:T(8,128)S(1)} %copy.22, f32[512]{0:T(512)S(1)} %fusion.10, f32[512]{0:T(512)S(1)} %broadcast_multiply_fusion.1, f32[512]{0:T(512)S(1)} %copy-done.9, f32[512,512]{1,0:T(8,128)S(1)} %get-tuple-element.35, ...), kind=kLoop, calls=%fused_computation.10 | loop fusion | flops 7862784 | bytes 5267456 | tf_op jit(solution)/shard_map/transpose(jvp())/reduce_sum | solution.py:24
  58.4 2.1 %convert_reduce_fusion = f32[1920]{0:T(1024)S(1)} fusion(bf16[512,1920]{1,0:T(8,128)(2,1)} %param.21, pred[512]{0:T(512)(128)(4,1)S(1)} %compare_reduce_fusion), kind=kLoop, calls=%fused_computation | loop fusion | flops 2947200 | bytes 1974272 | tf_op jit(solution)/shard_map/reduce_sum | solution.py:626
  60.6 5.0 %fusion.14 = f32[512,1920]{1,0:T(8,128)} fusion(bf16[512,1920]{1,0:T(8,128)(2,1)} %param.21, pred[512]{0:T(512)(128)(4,1)S(1)} %compare_reduce_fusion, f32[512,512]{1,0:T(8,128)S(1)} %copy-done.6, f32[512]{0:T(512)S(1)} %copy-done.13, f32[512]{0:T(512)S(1)} %copy-done.11, f32[512]{0:T(512)S(1)} %get-tuple-element.37, f32[512]{0:T(512)S(1)} %broadcast_multiply_fusion), kind=kOutput, calls=%fused_computation.56 | convolution fusion | flops 1008926720 | bytes 6955520 | tf_op jit(solution)/shard_map/dot_general | solution.py:33
  65.6 0.4 fusion.16
  66.2 0.8 fusion.8
  67.1 60.0 %reduce_all.1 = (bf16[512,512]{1,0:T(8,128)(2,1)S(1)}, f32[128,512]{1,0:T(8,128)S(1)}, f32[64,2048]{1,0:T(8,128)S(1)}, f32[8,8,128]{2,1,0:T(8,128)S(1)}) custom-call(bf16[512,512]{1,0:T(8,128)(2,1)S(1)} %add_convert_fusion.back_ref, f32[8,128,512]{2,1,0:T(8,128)S(1)} %bitcast.13, f32[8,64,1920]{2,1,0:T(8,128)} %bitcast.15, ...), custom_call_target="tpu_custom_call" | custom-call | tf_op jit(solution)/shard_map/reduce_all/pallas_call | solution.py:541
  127.0 1.6 %fusion = f32[256,1024]{1,0:T(8,128)} fusion(bf16[1024,512]{1,0:T(8,128)(2,1)S(1)} %get-tuple-element.15, bf16[512,256]{1,0:T(8,128)(2,1)S(1)} %get-tuple-element.17, bf16[512,512]{1,0:T(8,128)(2,1)S(1)} %get-tuple-element.18), kind=kOutput, calls=%fused_computation.7 | convolution fusion | flops 402784256 | bytes 2883584 | tf_op jit(solution)/shard_map/dot_general | solution.py:39
  128.7 0.8 slice.14
  129.5 0.6 reshape.97
  130.1 0.6 slice.17
  130.7 5.1 %add_select_fusion = f32[512,1920]{1,0:T(8,128)} fusion(bf16[512,1920]{1,0:T(8,128)(2,1)} %copy-done.3, f32[1920]{0:T(1024)S(1)} %copy-done.12, pred[512]{0:T(512)(128)(4,1)S(1)} %compare_reduce_fusion, f32[512,512]{1,0:T(8,128)} %copy-done.5, f32[512]{0:T(512)S(1)} %copy-done.13, f32[512]{0:T(512)S(1)} %copy-done.11, f32[512]{0:T(512)S(1)} %get-tuple-element.37, ...), kind=kOutput, calls=%fused_computation.1 | convolution fusion | flops 1009909760 | bytes 6963200 | tf_op jit(solution)/shard_map/dot_general | solution.py:617
  135.8 0.7 copy.29
  (41 shorter events, 0.4 us)
Async XLA Ops:
  2.1 1.0 copy-start
  3.1 0.9 copy-start.1
  4.1 0.9 copy-start.2
  47.3 2.0 %copy-start.3 = (bf16[512,1920]{1,0:T(8,128)(2,1)}, bf16[512,1920]{1,0:T(8,128)(2,1)S(1)}, u32[]{:S(2)}) copy-start(bf16[512,1920]{1,0:T(8,128)(2,1)S(1)} %get-tuple-element.16) | copy-start | bytes 5898244
  49.2 1.9 %copy-start.9 = (f32[512]{0:T(512)S(1)}, f32[512]{0:T(512)}, u32[]{:S(2)}) copy-start(f32[512]{0:T(512)} %param.15) | copy-start | bytes 6148
  49.2 1.9 %copy-start.10 = (f32[512]{0:T(512)S(1)}, f32[512]{0:T(512)}, u32[]{:S(2)}) copy-start(f32[512]{0:T(512)} %param.16) | copy-start | bytes 6148
  50.8 3.3 %copy-start.4 = (bf16[512,1920]{1,0:T(8,128)(2,1)S(1)}, bf16[512,1920]{1,0:T(8,128)(2,1)}, u32[]{:S(2)}) copy-start(bf16[512,1920]{1,0:T(8,128)(2,1)} %copy-done.3) | copy-start | bytes 5898244
  50.8 3.3 %copy-start.8 = (bf16[512,1920]{1,0:T(8,128)(2,1)S(1)}, bf16[512,1920]{1,0:T(8,128)(2,1)}, u32[]{:S(2)}) copy-start(bf16[512,1920]{1,0:T(8,128)(2,1)} %param.21) | copy-start | bytes 5898244
  50.9 3.3 %copy-start.11 = (f32[512]{0:T(512)S(1)}, f32[512]{0:T(512)}, u32[]{:S(2)}) copy-start(f32[512]{0:T(512)} %param.17) | copy-start | bytes 6148
  54.1 2.1 %copy-start.5 = (f32[512,512]{1,0:T(8,128)}, f32[512,512]{1,0:T(8,128)S(1)}, u32[]{:S(2)}) copy-start(f32[512,512]{1,0:T(8,128)S(1)} %get-tuple-element.34) | copy-start | bytes 3145732
  58.4 2.2 %copy-start.13 = (f32[512]{0:T(512)S(1)}, f32[512]{0:T(512)}, u32[]{:S(2)}) copy-start(f32[512]{0:T(512)} %param.18) | copy-start | bytes 6148
  58.4 2.2 %copy-start.6 = (f32[512,512]{1,0:T(8,128)S(1)}, f32[512,512]{1,0:T(8,128)}, u32[]{:S(2)}) copy-start(f32[512,512]{1,0:T(8,128)} %copy-done.5) | copy-start | bytes 3145732
  60.6 5.0 %copy-start.7 = (f32[512,512]{1,0:T(8,128)S(1)}, f32[512,512]{1,0:T(8,128)}, u32[]{:S(2)}) copy-start(f32[512,512]{1,0:T(8,128)} %get-tuple-element.32) | copy-start | bytes 3145732
  127.0 3.7 %copy-start.12 = (f32[1920]{0:T(1024)S(1)}, f32[1920]{0:T(1024)}, u32[]{:S(2)}) copy-start(f32[1920]{0:T(1024)} %param.20) | copy-start | bytes 23044

commit v2 on v0

v2 whole, which is shorter than its diff:
```python
import functools
import math

import jax
import jax.numpy as jnp
from jax import lax
from jax.experimental import pallas as pl
from jax.experimental.pallas import tpu as pltpu
from jax.sharding import PartitionSpec as P

CAP = 2
SEG = 8
UNIT = CAP * SEG
GROUP = 8
TILE = GROUP * UNIT
SUB = 32
MARK = 64.0
FIRST = 1152
KEEP = 32
MESH = pl.DeviceIdType.MESH

epsilon = 1e-05


def remote(src, dst, send, recv, device):
    return pltpu.make_async_remote_copy(
        src_ref=src,
        dst_ref=dst,
        send_sem=send,
        recv_sem=recv,
        device_id=device,
        device_id_type=MESH,
    )


def loop(first, last, body):
    def step(index, carry):
        body(index)
        return carry

    lax.fori_loop(first, last, step, 0)


def span(index, size):
    return pl.ds(pl.multiple_of(index * size, size), size)


def product(left, right, left_dim=1, right_dim=0):
    return lax.dot_general(
        left, right, (((left_dim,), (right_dim,)), ((), ())), preferred_element_type=jnp.float32
    )


def row_mean(values):
    return jnp.mean(values, axis=-1, keepdims=True)


def to_column(row):
    size = row.shape[1]
    down = lax.broadcasted_iota(jnp.int32, (size, size), 0)
    across = lax.broadcasted_iota(jnp.int32, (size, size), 1)
    spread = jnp.broadcast_to(row, (size, size))
    return jnp.sum(jnp.where(down == across, spread, 0.0), axis=1, keepdims=True)


def slot_targets(dest, live, frames):
    segments = frames // SEG
    seg = lax.broadcasted_iota(jnp.int32, (segments, frames), 0)
    frame = lax.broadcasted_iota(jnp.int32, (segments, frames), 1)
    owner = frame // SEG
    mine = owner == seg
    dest_all = jnp.broadcast_to(to_column(dest.astype(jnp.float32)), (segments, frames))
    live_all = jnp.broadcast_to(to_column(live.astype(jnp.float32)), (segments, frames))
    dest_row = jnp.sum(jnp.where(mine, dest_all, 0.0), axis=0, keepdims=True)
    live_row = jnp.sum(jnp.where(mine, live_all, 0.0), axis=0, keepdims=True)
    same = jnp.where(dest_all == dest_row, 1.0, 0.0)
    rank = jnp.sum(jnp.where(seg < owner, same, 0.0), axis=0, keepdims=True)
    position = (lax.broadcasted_iota(jnp.int32, (1, frames), 1) % SEG).astype(jnp.float32)
    row = (dest_row * CAP + rank) * SEG + position
    return jnp.where(position < live_row, row, -1.0)


def fold_rows(values):
    rows, cols = values.shape
    return jnp.sum(values.reshape(rows // 8, 8, cols), axis=0)


def tail_both(hidden, back, gain1, shift1, gain2, shift2):
    centred = hidden - row_mean(hidden)
    rate1 = lax.rsqrt(row_mean(centred * centred) + epsilon)
    norm1 = centred * rate1
    value = norm1 * gain1 + shift1
    cdf = 0.5 + 0.5 * lax.erf(value * (1.0 / math.sqrt(2.0)))
    active = value * cdf
    slope = cdf + value * (jnp.exp(value * value * -0.5) * (1.0 / math.sqrt(2.0 * math.pi)))
    centred2 = active - row_mean(active)
    rate2 = lax.rsqrt(row_mean(centred2 * centred2) + epsilon)
    norm2 = centred2 * rate2
    features = norm2 * gain2 + shift2
    d_norm2 = back * gain2
    back_active = rate2 * (d_norm2 - row_mean(d_norm2) - norm2 * row_mean(d_norm2 * norm2))
    back_value = back_active * slope
    d_norm1 = back_value * gain1
    back_hidden = rate1 * (d_norm1 - row_mean(d_norm1) - norm1 * row_mean(d_norm1 * norm1))
    return features, back_hidden, (back_value * norm1, back_value, back * norm2, back)

def exchange_kernel(
    n_dp,
    n_par,
    scale,
    conv_hbm,
    dest_ref,
    live_ref,
    wc_ref,
    wp_ref,
    cot_hbm,
    gain1_ref,
    shift1_ref,
    gain2_ref,
    shift2_ref,
    wc_hbm,
    wp_hbm,
    feat_hbm,
    mine_out,
    oc,
    op,
    osm,
    conv_in,
    cot,
    cot_m,
    wc_full,
    wp_full,
    packed,
    x_all,
    x_m,
    live_all,
    back_raw,
    hid,
    feat,
    feat_out,
    back_tile,
    ft,
    fm,
    lt,
    bt,
    bm,
    back,
    norm_acc,
    bias_row,
    gp1,
    gp2,
    gc1,
    gc2,
    r1p,
    r1c,
    r2p,
    r2c,
    t1p,
    t1c,
    t2p,
    t2c,
    u1p,
    u1c,
    u2p,
    u2c,
    sp,
    sc,
    cp,
    cc,
    small,
    small_m,
    sq,
    sr,
    ret,
    load_sem,
    store_sem,
    x_send,
    x_recv,
    w_send,
    w_recv,
    f_send,
    f_recv,
    b_send,
    b_recv,
    m_send,
    m_recv,
    a_send,
    a_recv,
    z_send,
    z_recv,
    s_send,
    s_recv,
    g_send,
    g_recv,
    k_send,
    k_recv,
):
    f32, b16 = jnp.float32, jnp.bfloat16
    me_dp, me_par = lax.axis_index("dp"), lax.axis_index("param")
    core = lax.rem(me_dp, 2)
    mate = me_dp + 1 - 2 * core
    me_chip = me_dp // 2
    n_chip = n_dp // 2
    n_z = n_chip // 2
    n_y = n_par // 2
    me_z = lax.rem(me_chip, n_z)
    x_hi = me_chip // n_z
    y, x_lo = me_par // 2, lax.rem(me_par, 2)
    x_me = x_lo * 2 + x_hi
    n_group = n_dp // GROUP
    me_group, me_in = me_dp // GROUP, lax.rem(me_dp, GROUP)
    frames = conv_in.shape[0]
    slots = x_all.shape[0]
    channels = gain1_ref.shape[1]
    model = cot.shape[1]

    def dp_at(k):
        return lax.rem(me_group + k // GROUP, n_group) * GROUP + lax.rem(
            me_in + lax.rem(k, GROUP), GROUP
        )

    def dp_from(k):
        return lax.rem(me_group - k // GROUP + n_group, n_group) * GROUP + lax.rem(
            me_in - lax.rem(k, GROUP) + GROUP, GROUP
        )

    def y_at(k):
        return lax.rem(y + k, n_y)

    def y_from(k):
        return lax.rem(y + n_y - k, n_y)

    def y_peer(k):
        return (me_dp, y_at(k) * 2 + x_lo)

    def x_at(k):
        low = 1 - x_lo if k & 2 else x_lo
        high = 1 - x_hi if k & 1 else x_hi
        return low, high

    def x_peer(k):
        low, high = x_at(k)
        return ((high * n_z + me_z) * 2 + core, y * 2 + low)

    def x_place(k):
        low, high = x_at(k)
        return low * 2 + high

    def z_peer(k):
        return ((x_hi * n_z + lax.rem(me_z + k, n_z)) * 2 + core, me_par)

    ours = (mate, me_par)

    shards = ((wc_ref, wc_full), (wp_ref, wp_full))
    loads = [
        pltpu.make_async_copy(conv_hbm, conv_in, load_sem.at[0]),
        pltpu.make_async_copy(cot_hbm, cot, load_sem.at[1]),
    ]
    for w, (shard, full) in enumerate(shards):
        rows = full.at[span(me_par, shard.shape[0])]
        loads.append(pltpu.make_async_copy(shard, rows, load_sem.at[2 + w]))
    for load in loads:
        load.start()
    barrier = pltpu.get_barrier_semaphore()

    def greet(device):
        pl.semaphore_signal(barrier, inc=1, device_id=device, device_id_type=MESH)

    loop(1, n_dp, lambda k: greet((dp_at(k), me_par)))
    loop(1, n_y, lambda k: greet(y_peer(k)))
    greet(x_peer(2))
    greet(x_peer(3))

    target = slot_targets(dest_ref[...], live_ref[...], frames)
    loads[0].wait()

    def pack(t):
        rows = span(t, TILE)
        here = (lax.broadcasted_iota(jnp.int32, (TILE, frames), 0) + t * TILE).astype(f32)
        hit = jnp.where(here == target, 1.0, 0.0)
        empty = 1.0 - jnp.sum(hit, axis=1, keepdims=True)
        moved = product(hit.astype(b16), conv_in[...])
        packed[rows, :] = (moved + empty * MARK).astype(b16)

    loop(0, slots // TILE, pack)
    pl.semaphore_wait(barrier, n_dp + n_y)

    own_steps = [1] + [2 * k for k in range(1, n_y)]
    far_steps = [2 * k + 1 for k in range(1, n_y)]

    def weight_rows(w, s, which):
        shard, full = shards[w]
        flip = lax.rem(s, 2)
        low = x_lo + flip - 2 * flip * x_lo
        owner = y_from(s // 2) * 2 + low
        return full.at[span(owner * 2 + which, shard.shape[0] // 2)]

    def send_weight(w, s):
        shard, full = shards[w]
        half = shard.shape[0] // 2
        low = 1 - x_lo if s in far_steps else x_lo
        place = full.at[span((y * 2 + low) * 2 + core, half)]
        source = place if s in far_steps else shard.at[span(core, half)]
        device = x_peer(2) if s == 1 else y_peer(s // 2)
        return remote(source, place, w_send.at[w, s], w_recv.at[w, s], device)

    def await_weight(w, s):
        rows = weight_rows(w, s, core)
        remote(rows, rows, w_send.at[w, s], w_recv.at[w, s], ours).wait_recv()

    def pass_on(w, s, which):
        rows = weight_rows(w, s, which)
        return remote(rows, rows, f_send.at[w, s], f_recv.at[w, s], ours)

    def send_rows(k):
        to = dp_at(k)
        return remote(
            packed.at[span(to, UNIT)],
            x_all.at[span(me_dp, UNIT)],
            x_send.at[k],
            x_recv.at[k],
            (to, me_par),
        )

    def recv_rows(k):
        source = dp_from(k)
        rows = x_all.at[span(source, UNIT)]
        return remote(rows, rows, x_send.at[k], x_recv.at[k], (source, me_par))

    for w in range(2):
        for s in own_steps:
            send_weight(w, s).start()
    loop(1, n_dp, lambda k: send_rows(k).start())
    cot_share = remote(cot_hbm, cot_m, k_send.at[0], k_recv.at[0], ours)
    cot_share.start()
    x_all[span(me_dp, UNIT), :] = packed[span(me_dp, UNIT), :]
    for w in range(2):
        await_weight(w, 1)
        for s in far_steps:
            send_weight(w, s).start()
        pass_on(w, 1, core).start()
    for w in range(2):

        def relay(s):
            await_weight(w, s)
            pass_on(w, s, core).start()

        loop(2, 2 * n_y, relay)
    for w in range(2):
        loop(1, 2 * n_y, lambda s: pass_on(w, s, 1 - core).wait_recv())
    for load in loads[1:]:
        load.wait()
    keep_weights = [
        pltpu.make_async_copy(wc_full, wc_hbm, store_sem.at[n_group]),
        pltpu.make_async_copy(wp_full, wp_hbm, store_sem.at[n_group + 1]),
    ]
    for copy in keep_weights:
        copy.start()

    def back_product(t):
        rows = span(t, TILE)
        back_raw[rows, :] = product(cot[rows, :], wp_full[...], 1, 1)

    loop(0, slots // TILE, back_product)
    norm_acc[...] = jnp.zeros_like(norm_acc)

    def tile_rows(t):
        return span(lax.rem(me_group - t + n_group, n_group), TILE)

    def store_rows(t):
        rows = tile_rows(t)
        return pltpu.make_async_copy(feat_out.at[rows], feat_hbm.at[rows], store_sem.at[t])

    def mate_x(t):
        rows = tile_rows(t)
        return remote(x_all.at[rows], x_m.at[rows], m_send.at[0, t], m_recv.at[0, t], ours)

    def mate_feat(t):
        cols = tile_rows(t)
        return remote(
            ft.at[:, 1 - core, :, cols], fm.at[:, :, cols], m_send.at[1, t], m_recv.at[1, t], ours
        )

    def mate_back(t):
        cols = tile_rows(t)
        return remote(
            bt.at[1 - core, :, cols], bm.at[:, cols], m_send.at[2, t], m_recv.at[2, t], ours
        )

    def tile(t):
        group = lax.rem(me_group - t + n_group, n_group)
        rows = tile_rows(t)
        loop(jnp.maximum(1, t * GROUP), (t + 1) * GROUP, lambda k: recv_rows(k).wait_recv())
        arrived = x_all[rows, :]
        live = jnp.where(arrived[:, :1].astype(f32) < MARK / 2, 1.0, 0.0)
        live_all[rows, :] = jnp.broadcast_to(live, (TILE, 128))
        kept = arrived * live.astype(b16)
        x_all[rows, :] = kept
        mate_x(t).start()
        hid[...] = product(kept, wc_full[...])

        def few(u):
            sub = span(u, SUB)
            here = pl.ds(pl.multiple_of(group * TILE + u * SUB, SUB), SUB)
            keep = live_all[here, :][:, :1]
            features, grad, terms = tail_both(
                hid[sub, :],
                back_raw[here, :] * keep,
                gain1_ref[...],
                shift1_ref[...],
                gain2_ref[...],
                shift2_ref[...],
            )
            feat[sub, :] = features * keep
            back_tile[sub, :] = grad
            for n, term in enumerate(terms):
                norm_acc[n] += fold_rows(term)

        loop(0, TILE // SUB, few)
        ft[:, :, :, rows] = feat[...].T.astype(b16).reshape(ft.shape[:3] + (TILE,))
        mate_feat(t).start()
        bt[:, :, rows] = back_tile[...].T.astype(b16).reshape(bt.shape[:2] + (TILE,))
        mate_back(t).start()
        lt[:, rows] = live_all[rows, :].T[: lt.shape[0]].astype(b16)
        back[rows, :] = back_tile[...].astype(b16)
        feat_out[rows, :channels] = feat[...].astype(b16)
        feat_out[rows, channels:] = live_all[rows, :].astype(b16)
        store_rows(t).start()

    loop(0, n_group, tile)

    half = channels // 2
    loop(0, n_group, lambda t: mate_feat(t).wait_recv())
    cot_share.wait_recv()
    step = 384

    def proj_part(cols):
        left = jnp.concatenate([ft[:, core].reshape(half, slots), lt[...]], axis=0)
        own = product(left, cot[:, cols])
        bias_row[:, cols] = own[half : half + 1]
        both = own[:half] + product(fm[...].reshape(half, slots), cot_m[:, cols])
        return both.astype(b16).reshape(n_y, 4, half // n_par // 2, step)

    def proj_first(n):
        gp1[:, :, :, span(n, step)] = proj_part(span(n, step))

    def proj_second(n):
        gp2[:, :, :, span(n, step)] = proj_part(
            pl.ds(pl.multiple_of(n * step + FIRST, 128), step)
        )

    def first_y(k, w):
        held, landing = ((gp1, r1p), (gc1, r1c))[w]
        return remote(
            held.at[y_at(k)], landing.at[k], a_send.at[w, k], a_recv.at[w, k], y_peer(k)
        )

    def second_x(k, w):
        held, landing = ((gp2, r2p), (gc2, r2c))[w]
        return remote(
            held.at[:, x_place(k)],
            landing.at[k],
            a_send.at[2 + w, k],
            a_recv.at[2 + w, k],
            x_peer(k),
        )

    offsets = range(1, 4)
    loop(0, FIRST // step, proj_first)
    for k in offsets:
        first_y(k, 0).start()
    loop(0, (model - FIRST) // step, proj_second)
    for k in offsets:
        second_x(k, 0).start()

    loop(0, n_group, lambda t: mate_back(t).wait_recv())
    loop(0, n_group, lambda t: mate_x(t).wait_recv())
    width = oc.shape[1]
    rest = half // 2 - KEEP

    def conv_part(n):
        cols = span(n, 2 * width)
        pair = product(bt[core], x_all[:, cols]) + product(bm[...], x_m[:, cols])
        pair = pair.astype(b16)
        for low in range(2):
            block = pair[:, low * width : (low + 1) * width]
            for high in range(2):
                top = high * (half // 2)
                gc1[n, low * 2 + high] = block[top : top + KEEP]
                gc2[n, low * 2 + high] = block[top + KEEP : top + KEEP + rest]

    loop(0, n_y, conv_part)
    for k in offsets:
        first_y(k, 1).start()
    for k in offsets:
        second_x(k, 1).start()

    lanes = 128
    per = channels // lanes
    small[...] = jnp.zeros_like(small)
    for v in range(4):
        total = jnp.sum(norm_acc[v], axis=0, keepdims=True)
        for q in range(per):
            at = per * v + q
            small[at : at + 1, :] = total[:, q * lanes : (q + 1) * lanes]
    for q in range(model // lanes):
        at = per * 4 + q
        small[at : at + 1, :] = bias_row[:, q * lanes : (q + 1) * lanes]
    share_small = remote(small, small_m, k_send.at[1], k_recv.at[1], ours)
    share_small.start()

    def back_rows(k):
        to = dp_at(k)
        return remote(
            back.at[span(to, UNIT)],
            ret.at[span(me_dp, UNIT)],
            b_send.at[k],
            b_recv.at[k],
            (to, me_par),
        )

    def back_wait(k):
        source = dp_from(k)
        rows = ret.at[span(source, UNIT)]
        remote(rows, rows, b_send.at[k], b_recv.at[k], (source, me_par)).wait_recv()

    loop(1, n_dp, lambda k: back_rows(k).start())
    ret[span(me_dp, UNIT), :] = back[span(me_dp, UNIT), :]

    few_rows = small.shape[0] // 2

    def small_step(stage, k):
        device = (y_peer, x_peer, z_peer)[stage](k)
        return remote(
            sq.at[stage], sr.at[stage, k], s_send.at[stage, k], s_recv.at[stage, k], device
        )

    def small_sum(stage, count):
        total = sq[stage]
        for k in range(1, count):
            small_step(stage, k).wait_recv()
            total = total + sr[stage, k]
        return total

    share_small.wait_recv()
    sq[0] = small[span(core, few_rows), :] + small_m[span(core, few_rows), :]
    for k in offsets:
        small_step(0, k).start()

    def then_x(k, w):
        held, landing = ((t1p, u1p), (t1c, u1c))[w]
        return remote(
            held.at[x_place(k)], landing.at[k], a_send.at[4 + w, k], a_recv.at[4 + w, k], x_peer(k)
        )

    def then_y(k, w):
        held, landing = ((t2p, u2p), (t2c, u2c))[w]
        return remote(
            held.at[y_at(k)], landing.at[k], a_send.at[6 + w, k], a_recv.at[6 + w, k], y_peer(k)
        )

    for k in offsets:
        first_y(k, 0).wait_recv()
    total = gp1[y].astype(f32)
    for k in offsets:
        total = total + r1p[k].astype(f32)
    t1p[...] = total
    for k in offsets:
        then_x(k, 0).start()
    for k in offsets:
        second_x(k, 0).wait_recv()
    total = gp2[:, x_me].astype(f32)
    for k in offsets:
        total = total + r2p[k].astype(f32)
    t2p[...] = total
    for k in offsets:
        then_y(k, 0).start()
    for k in offsets:
        first_y(k, 1).wait_recv()
    total = gc1[y].astype(f32)
    for k in offsets:
        total = total + r1c[k].astype(f32)
    t1c[...] = total
    for k in offsets:
        then_x(k, 1).start()
    for k in offsets:
        second_x(k, 1).wait_recv()
    total = gc2[:, x_me].astype(f32)
    for k in offsets:
        total = total + r2c[k].astype(f32)
    t2c[...] = total
    for k in offsets:
        then_y(k, 1).start()
    sq[1] = small_sum(0, 4)
    for k in offsets:
        small_step(1, k).start()

    sp[:, model:] = jnp.zeros((sp.shape[0], sp.shape[1] - model), f32)
    for k in offsets:
        then_x(k, 0).wait_recv()
    sp[:, :FIRST] = t1p[x_me] + u1p[1] + u1p[2] + u1p[3]
    for k in offsets:
        then_y(k, 0).wait_recv()
    sp[:, FIRST:model] = t2p[y] + u2p[1] + u2p[2] + u2p[3]
    for k in offsets:
        then_x(k, 1).wait_recv()
    sc[:KEEP, :] = t1c[x_me] + u1c[1] + u1c[2] + u1c[3]
    for k in offsets:
        then_y(k, 1).wait_recv()
    sc[KEEP:, :] = t2c[y] + u2c[1] + u2c[2] + u2c[3]

    wide = sp.shape[1] // n_z
    tall = sc.shape[0] // n_z

    def over_z(k, w):
        to = lax.rem(me_z + k, n_z)
        held = sp.at[:, span(to, wide)] if w == 0 else sc.at[span(to, tall)]
        landing = cp if w == 0 else cc
        return remote(held, landing.at[k], z_send.at[w, k], z_recv.at[w, k], z_peer(k))

    def start_z(k):
        over_z(k, 0).start()
        over_z(k, 1).start()

    loop(1, n_z, start_z)
    sq[2] = small_sum(1, 4)
    for k in range(1, n_z):
        small_step(2, k).start()

    def proj_place(chip):
        return (
            span(core * 2 + chip // n_z, sp.shape[0]),
            span(lax.rem(chip, n_z), wide),
        )

    def conv_place(chip):
        return span(core * n_chip + chip, tall)

    def wait_z(k):
        over_z(k, 0).wait_recv()
        over_z(k, 1).wait_recv()

    loop(1, n_z, wait_z)
    total = sp[:, span(me_z, wide)]
    for k in range(1, n_z):
        total = total + cp[k]
    op[proj_place(me_chip)] = total * scale
    total = sc[span(me_z, tall), :]
    for k in range(1, n_z):
        total = total + cc[k]
    oc[conv_place(me_chip), :] = total * scale

    def chip_at(k):
        return lax.rem(me_chip + k, n_chip)

    def chip_from(k):
        return lax.rem(me_chip + n_chip - k, n_chip)

    def share(w, k, chip, other):
        rows = op.at[proj_place(chip)] if w == 0 else oc.at[conv_place(chip)]
        return remote(rows, rows, g_send.at[w, k], g_recv.at[w, k], (other * 2 + core, me_par))

    def start_share(k):
        share(0, k, me_chip, chip_at(k)).start()
        share(1, k, me_chip, chip_at(k)).start()

    loop(1, n_chip, start_share)
    osm[span(core, few_rows), :] = small_sum(2, n_z) * scale

    def to_core(w, which):
        held = (op, oc, osm)[w]
        rows = held.at[span(which, held.shape[0] // 2)]
        return remote(rows, rows, k_send.at[2 + w], k_recv.at[2 + w], ours)

    to_core(2, core).start()

    loop(1, n_dp, back_wait)
    column = to_column(target)
    part = frames // 2
    for h in range(2):
        slot = lax.broadcasted_iota(jnp.int32, (part, slots), 1).astype(f32)
        pick = jnp.where(slot == column[h * part : (h + 1) * part], 1.0, 0.0).astype(b16)
        mine_out[h * part : (h + 1) * part, :] = product(pick, ret[...]).astype(b16)

    def weight_end(s):
        for w in range(2):
            pass_on(w, s, core).wait_send()

    loop(1, 2 * n_y, weight_end)
    for w in range(2):
        for s in own_steps + far_steps:
            send_weight(w, s).wait_send()
    for k in offsets:
        for w in range(2):
            first_y(k, w).wait_send()
            second_x(k, w).wait_send()
            then_x(k, w).wait_send()
            then_y(k, w).wait_send()
    for stage, count in ((0, 4), (1, 4), (2, n_z)):
        for k in range(1, count):
            small_step(stage, k).wait_send()

    def tile_end(t):
        mate_x(t).wait_send()
        mate_feat(t).wait_send()
        mate_back(t).wait_send()
        store_rows(t).wait()

    loop(0, n_group, tile_end)
    for copy in keep_weights:
        copy.wait()
    cot_share.wait_send()
    share_small.wait_send()

    def z_end(k):
        over_z(k, 0).wait_send()
        over_z(k, 1).wait_send()

    loop(1, n_z, z_end)

    def dp_end(k):
        send_rows(k).wait_send()
        back_rows(k).wait_send()

    loop(1, n_dp, dp_end)

    def end_share(k):
        share(0, k, chip_from(k), chip_from(k)).wait_recv()
        share(1, k, chip_from(k), chip_from(k)).wait_recv()

    loop(1, n_chip, end_share)
    to_core(0, core).start()
    to_core(1, core).start()

    def chip_end(k):
        for w in range(2):
            share(w, k, me_chip, chip_at(k)).wait_send()

    loop(1, n_chip, chip_end)
    for w in range(3):
        to_core(w, 1 - core).wait_recv()
        to_core(w, core).wait_send()


def finish_kernel(
    feat_ref,
    wp_ref,
    bias_ref,
    mine_ref,
    wc_ref,
    oc_ref,
    op_ref,
    osm_ref,
    projected_ref,
    frames_ref,
    conv_out,
    proj_out,
    norm_out,
    bias_out,
):
    channels = wp_ref.shape[0]
    model = wp_ref.shape[1]
    live = feat_ref[:, channels : channels + 1].astype(jnp.float32)
    lifted = product(feat_ref[:, :channels], wp_ref[...]) + bias_ref[...].reshape(1, model)
    projected_ref[...] = lifted * live
    frames_ref[...] = product(mine_ref[...], wc_ref[...], 1, 1)

    @pl.when(pl.program_id(0) == 0)
    def _():
        lanes = osm_ref.shape[1]
        per = channels // lanes
        conv_out[...] = oc_ref[...].T
        proj_out[...] = op_ref[:, :model]
        for v in range(4):
            for q in range(per):
                at = per * v + q
                norm_out[v : v + 1, q * lanes : (q + 1) * lanes] = osm_ref[at : at + 1, :]
        for q in range(model // lanes):
            bias_out[q * lanes : (q + 1) * lanes] = osm_ref[4 * per + q, :]


def on_device(
    conv_input,
    block_dest,
    live_frames,
    conv_weight,
    conv_gain,
    conv_shift,
    feat_gain,
    feat_shift,
    proj_weight,
    proj_bias,
    cotangent,
):
    n_dp = lax.axis_size("dp")
    n_par = lax.axis_size("param")
    n_chip = n_dp // 2
    n_z = n_chip // 2
    n_y = n_par // 2
    n_group = n_dp // GROUP
    frames, width = conv_input.shape
    slots = n_dp * UNIT
    channels = conv_gain.shape[0]
    model = proj_bias.shape[0]
    conv_rows, proj_rows = conv_weight.shape[0], proj_weight.shape[0]
    padded = -(-model // (128 * n_z)) * 128 * n_z
    hp = proj_rows // 4
    hc = channels // 4
    second = model - FIRST
    scale = 1.0 / math.sqrt(frames * n_dp * n_par)
    f32, b16 = jnp.float32, jnp.bfloat16
    vmem = pl.BlockSpec(memory_space=pltpu.VMEM)
    hbm = pl.BlockSpec(memory_space=pl.ANY)
    dma = pltpu.SemaphoreType.DMA
    buf = pltpu.VMEM
    out = jax.ShapeDtypeStruct
    wc_full, wp_full, feat, mine, oc, op, osm = pl.pallas_call(
        functools.partial(exchange_kernel, n_dp, n_par, scale),
        out_shape=(
            out((width, channels), b16),
            out((channels, model), b16),
            out((slots, channels + 128), b16),
            out((frames, channels), b16),
            out((channels, conv_rows), f32),
            out((proj_rows, padded), f32),
            out((32, 128), f32),
        ),
        in_specs=[hbm, vmem, vmem, hbm, hbm, hbm, vmem, vmem, vmem, vmem],
        out_specs=(hbm, hbm, hbm, vmem, vmem, vmem, vmem),
        scratch_shapes=[
            buf((frames, width), b16),
            buf((slots, model), b16),
            buf((slots, model), b16),
            buf((width, channels), b16),
            buf((channels, model), b16),
            buf((slots, width), b16),
            buf((slots, width), b16),
            buf((slots, width), b16),
            buf((slots, 128), f32),
            buf((slots, channels), f32),
            buf((TILE, channels), f32),
            buf((TILE, channels), f32),
            buf((slots, channels + 128), b16),
            buf((TILE, channels), f32),
            buf((n_par, 2, proj_rows // 2, slots), b16),
            buf((n_par, proj_rows // 2, slots), b16),
            buf((16, slots), b16),
            buf((2, channels // 2, slots), b16),
            buf((channels // 2, slots), b16),
            buf((slots, channels), b16),
            buf((4, 8, channels), f32),
            buf((1, model), f32),
            buf((n_y, 4, hp, FIRST), b16),
            buf((n_y, 4, hp, second), b16),
            buf((n_y, 4, KEEP, conv_rows), b16),
            buf((n_y, 4, hc - KEEP, conv_rows), b16),
            buf((4, 4, hp, FIRST), b16),
            buf((4, 4, KEEP, conv_rows), b16),
            buf((4, n_y, hp, second), b16),
            buf((4, n_y, hc - KEEP, conv_rows), b16),
            buf((4, hp, FIRST), f32),
            buf((4, KEEP, conv_rows), f32),
            buf((n_y, hp, second), f32),
            buf((n_y, hc - KEEP, conv_rows), f32),
            buf((4, hp, FIRST), f32),
            buf((4, KEEP, conv_rows), f32),
            buf((4, hp, second), f32),
            buf((4, hc - KEEP, conv_rows), f32),
            buf((hp, padded), f32),
            buf((hc, conv_rows), f32),
            buf((n_z, hp, padded // n_z), f32),
            buf((n_z, hc // n_z, conv_rows), f32),
            buf((32, 128), f32),
            buf((32, 128), f32),
            buf((3, 16, 128), f32),
            buf((3, n_z, 16, 128), f32),
            buf((slots, channels), b16),
            dma((4,)),
            dma((n_group + 2,)),
            dma((n_dp,)),
            dma((n_dp,)),
            dma((2, n_par)),
            dma((2, n_par)),
            dma((2, n_par)),
            dma((2, n_par)),
            dma((n_dp,)),
            dma((n_dp,)),
            dma((3, n_group)),
            dma((3, n_group)),
            dma((8, 4)),
            dma((8, 4)),
            dma((2, n_z)),
            dma((2, n_z)),
            dma((3, n_z)),
            dma((3, n_z)),
            dma((2, n_chip)),
            dma((2, n_chip)),
            dma((5,)),
            dma((5,)),
        ],
        compiler_params=pltpu.CompilerParams(
            collective_id=0, has_side_effects=True, vmem_limit_bytes=56 * 1024 * 1024
        ),
        name="exchange",
    )(
        conv_input,
        block_dest.reshape(1, -1),
        live_frames.reshape(1, -1),
        conv_weight,
        proj_weight,
        cotangent,
        conv_gain.reshape(1, -1),
        conv_shift.reshape(1, -1),
        feat_gain.reshape(1, -1),
        feat_shift.reshape(1, -1),
    )
    steps = 4

    def fixed(array):
        return pl.BlockSpec(array.shape, lambda i: (0,) * array.ndim)

    def rows_of(count, cols):
        return pl.BlockSpec((count // steps, cols), lambda i: (i, 0))

    outs = (
        out((slots, model), f32),
        out((frames, width), f32),
        out((conv_rows, channels), f32),
        out((proj_rows, model), f32),
        out((4, channels), f32),
        out((model,), f32),
    )
    return pl.pallas_call(
        finish_kernel,
        grid=(steps,),
        out_shape=outs,
        in_specs=[
            rows_of(slots, channels + 128),
            fixed(wp_full),
            fixed(proj_bias),
            rows_of(frames, channels),
            fixed(wc_full),
            fixed(oc),
            fixed(op),
            fixed(osm),
        ],
        out_specs=(rows_of(slots, model), rows_of(frames, width)) + tuple(fixed(o) for o in outs[2:]),
        compiler_params=pltpu.CompilerParams(vmem_limit_bytes=56 * 1024 * 1024),
        name="finish",
    )(feat, wp_full, proj_bias, mine, wc_full, oc, op, osm)


def solution(mesh):
    return jax.shard_map(
        on_device,
        mesh=mesh,
        in_specs=(
            P(("dp", "param"), None),
            P(("dp", "param"), None),
            P(("dp", "param")),
            P("param", None),
            P(),
            P(),
            P(),
            P(),
            P("param", None),
            P(),
            P(("dp", "param"), None),
        ),
        out_specs=(
            P(("dp", "param"), None),
            P(("dp", "param"), None),
            P("param", None),
            P("param", None),
            P(),
            P(),
        ),
        check_vma=False,
    )
```

time: 577 us -> 104 us (0.18)
  waiting for transfers between devices: 393 us -> 0 us
  Pallas kernels: 0 us -> 103 us
  blocking collectives: 92 us -> 0 us
  starting transfers between devices: 27.7 us -> 0 us
  matrix products: 22.3 us -> 0 us
  other arithmetic: 14.4 us -> 0 us
  between operations: 14 us -> 0.64 us
  local copies, waits for them, and re-layouts: 11.1 us -> 0 us
    psum x1 -> x0, waiting for transfers between devices: 257 us -> none  [project_backward(): replica = lax.psum((conv_grad, proj_grad), 'dp')]
    pallas_call x0 -> x2, Pallas kernels: none -> 103 us  [the longest x1 96.1 us: on_device(): pl.pallas_call(functools.partial(exchange_kernel, n_dp, n_par, scale), ou...]
    psum x1 -> x0, blocking collectives: 92 us -> none  [project_backward(): shared = lax.psum((norm_local, bias_local), ('dp', 'param'))]
    all_gather x2 -> x0, waiting for transfers between devices: 62.3 us -> none  [the longest x1 43.9 us: project_forward(): lax.all_gather(proj_weight, 'param', axis=0, tiled=True)]
    reduce_scatter x2 -> x0, waiting for transfers between devices: 57.1 us -> none  [the longest x1 57.1 us: project_backward(): lax.psum_scatter(contract_rows(window, upstream), 'param', scatter_dimens...]
    all_to_all x3 -> x0, starting transfers between devices: 27.3 us -> none  [the longest x1 12.6 us: on_device(): lax.all_to_all(slot_live, 'dp', split_axis=0, concat_axis=0, tiled=True)]
    dot_general x8 -> x0, matrix products: 22.3 us -> none  [the longest x2 7.03 us: contract_rows(): lax.dot_general(left, right, (((0,), (0,)), ((), ())), preferred_element_...]
    all_to_all x3 -> x0, waiting for transfers between devices: 14.5 us -> none  [the longest x1 8.41 us: on_device(): lax.all_to_all(sending.reshape(dp_count, CAP * segment, in_width), 'dp',...]
  transfers between devices with their start and end apart: 8 -> 0, of which waited for: 6 -> 0; matrix products, arithmetic and copies ran while one was open for 5% -> 0% of each run, Pallas kernels for 0% -> 0%
where the time goes in v2:
time: 104 us
  Pallas kernels  103 us (99%)
    pallas_call x1, Pallas kernels, on_device(): pl.pallas_call(functools.partial(exchange_kernel, n_dp, n_par, scale), ou...  96.1 us
    pallas_call x1, Pallas kernels, on_device(): pl.pallas_call(finish_kernel, grid=(steps,), out_shape=outs, in_specs=[ro...  7.27 us

profile of v2, /device:TPU:1, one launch (start us, length us, event | category | flops | bytes accessed | tf_op | source)
XLA Modules:
  0.0 104.0 jit_solution(18075062949290581715)
XLA Ops:
  0.6 96.1 %exchange.1 = (bf16[1024,512]{1,0:T(8,128)(2,1)}, bf16[512,1920]{1,0:T(8,128)(2,1)}, bf16[512,640]{1,0:T(8,128)(2,1)}, bf16[256,512]{1,0:T(8,128)(2,1)}, f32[512...) custom-call(bf16[256,1024]{1,0:T(8,128)(2,1)} %conv_hbm.1, s32[1,32]{1,0:T(1,128)} %bitcast.10, ...), custom_call_target="tpu_custom_call" | custom-call | tf_op jit(solution)/shard_map/exchange/pallas_call | solution.py:817
  96.7 7.3 %finish.1 = (f32[512,1920]{1,0:T(8,128)}, f32[256,1024]{1,0:T(8,128)}, f32[128,512]{1,0:T(8,128)}, f32[64,1920]{1,0:T(8,128)}, f32[4,512]{1,0:T(4,128)}, /*index=5*/f32[1920]{0:T(1024)}) custom-call(bf16[512,640]{1,0:T(8,128)(2,1)} %get-tuple-element.13.feat_ref, bf16[512,1920]{1,0:T(8,128)(2,1)} %get-tuple-element.14.wp_ref, f32[1920]{0:T(1024)} %bias_ref.1, ...), custom_call_target="tpu_custom_call" | custom-call | tf_op jit(solution)/shard_map/finish/pallas_call | solution.py:933
